TPU v7x, 512 devices: a whole 4x4x16 slice. The times are simulated.
512 devices in a mesh: fsdp: 32 (over z_lo, x), seq: 16 (over y, z_hi, core).
Axes of the slice: x: 4, y: 4, z: 16 (z_hi: 2, z_lo: 8; z = z_hi * 8 + z_lo), core: 2. Of those that a mesh axis runs over, the one named last changes fastest.
Arguments:
- query: bfloat16 [65536, 4096], P(('fsdp', 'seq')), may hold values from -8 to 8
- key: bfloat16 [65536, 1024], P(('fsdp', 'seq')), may hold values from -8 to 8
- value: bfloat16 [65536, 1024], P(('fsdp', 'seq')), may hold values from -6 to 6
- out_grad: bfloat16 [65536, 4096], P(('fsdp', 'seq')), may hold values from -24 to 24
- pack_order: int32 [32, 64], P('fsdp'), may hold values from 0 to 63, each once within a row
- doc_ids: int32 [32, 1, 2048], P('fsdp'), may hold values from 0 to 3, never falling along the last dimension, each value on 1 to 1024 neighbouring positions
Outputs:
- query_grad: bfloat16 [65536, 4096], P(('fsdp', 'seq'))
- key_grad: bfloat16 [65536, 1024], P(('fsdp', 'seq'))
- value_grad: bfloat16 [65536, 1024], P(('fsdp', 'seq'))
- bias_grads: float32 [5120], P('fsdp')
Inputs may be any that keep to these rules, and one draw needn't show every extreme that they name: `pack_order`: each row lists every block of its fsdp index exactly once. `doc_ids`: within a pack ids never fall; each of the 4 responses holds 1 to 1024 positions, and one holds exactly 1024.
All inputs are finite; a program needn't handle non-finite values.
Results may differ from a plain program's by a relative error of at most 0.025.
Values may be sent and summed in bfloat16 or wider, within the bound.
A program may use at most 128 MiB of HBM per device.

v0:
```python
import math

import jax
import jax.numpy as jnp
from jax import lax
from jax.sharding import PartitionSpec as P

QH = 32
KVH = 8
HD = 128


def block_gradients(
    query_block, grad_block, key_range, value_range, query_docs, key_docs, offset, scaling
):
    scores = (
        jnp.einsum("qgrd,kgd->grqk", query_block, key_range, preferred_element_type=jnp.float32)
        * scaling
    )
    query_pos = offset + jnp.arange(query_block.shape[0])
    key_pos = jnp.arange(key_range.shape[0])
    allowed = (key_pos[None, :] <= query_pos[:, None]) & (key_docs[None, :] == query_docs[:, None])
    scores = jnp.where(allowed, scores, -1e30)
    exponent = jnp.exp(scores - jnp.max(scores, axis=-1, keepdims=True))
    weights = (exponent / jnp.sum(exponent, axis=-1, keepdims=True)).astype(jnp.bfloat16)
    prob_grad = jnp.einsum(
        "qgrd,kgd->grqk", grad_block, value_range, preferred_element_type=jnp.float32
    )
    widened = weights.astype(jnp.float32)
    row_dot = jnp.sum(widened * prob_grad, axis=-1, keepdims=True)
    score_grad = (widened * (prob_grad - row_dot)).astype(jnp.bfloat16)
    query_piece = (
        jnp.einsum("grqk,kgd->qgrd", score_grad, key_range, preferred_element_type=jnp.float32)
        * scaling
    ).astype(jnp.bfloat16)
    key_part = (
        jnp.einsum("grqk,qgrd->kgd", score_grad, query_block, preferred_element_type=jnp.float32)
        * scaling
    )
    value_part = jnp.einsum(
        "grqk,qgrd->kgd", weights, grad_block, preferred_element_type=jnp.float32
    )
    return (query_piece, key_part, value_part)


def local(query, key, value, out_grad, pack_order, doc_ids):
    seq_count = lax.axis_size("seq")
    tok_rows = query.shape[0]
    head_dim = HD
    heads_here = QH // seq_count
    repeat_factor = max(1, seq_count // KVH)
    kv_here = max(1, KVH // seq_count)
    ratio = heads_here // kv_here
    group_rows = tok_rows * seq_count
    pack_count = 1
    query_split = query.reshape(tok_rows, seq_count, heads_here * head_dim)
    grad_split = out_grad.reshape(tok_rows, seq_count, heads_here * head_dim)
    key_slots = jnp.repeat(key.reshape(tok_rows, KVH, head_dim), repeat_factor, axis=1)
    value_slots = jnp.repeat(value.reshape(tok_rows, KVH, head_dim), repeat_factor, axis=1)
    query_heads, key_heads, value_heads, grad_heads = (
        lax.all_to_all(query_split, "seq", split_axis=1, concat_axis=0, tiled=True),
        lax.all_to_all(key_slots, "seq", split_axis=1, concat_axis=0, tiled=True),
        lax.all_to_all(value_slots, "seq", split_axis=1, concat_axis=0, tiled=True),
        lax.all_to_all(grad_split, "seq", split_axis=1, concat_axis=0, tiled=True),
    )
    order = pack_order[0]
    block_count = order.shape[0]
    pack_len = group_rows // pack_count

    def packed(rows):
        blocks = rows.reshape(block_count, -1, rows.shape[-1])
        return jnp.take(blocks, order, axis=0).reshape(pack_count, pack_len, rows.shape[-1])

    query_packed = packed(query_heads).reshape(pack_count, pack_len, kv_here, ratio, head_dim)
    grad_packed = packed(grad_heads).reshape(pack_count, pack_len, kv_here, ratio, head_dim)
    key_packed = packed(key_heads).reshape(pack_count, pack_len, kv_here, head_dim)
    value_packed = packed(value_heads).reshape(pack_count, pack_len, kv_here, head_dim)
    block_len = min(512, pack_len)
    scaling = 1.0 / math.sqrt(head_dim)
    query_list = []
    documents = doc_ids[0, 0]
    key_total = jnp.zeros((pack_len, kv_here, head_dim), jnp.float32)
    value_total = jnp.zeros((pack_len, kv_here, head_dim), jnp.float32)
    for block_index in range(pack_len // block_len):
        start = block_index * block_len
        finish = start + block_len
        query_piece, key_part, value_part = block_gradients(
            query_packed[0, start:finish],
            grad_packed[0, start:finish],
            key_packed[0, :finish],
            value_packed[0, :finish],
            documents[start:finish],
            documents[:finish],
            start,
            scaling,
        )
        query_list.append(query_piece.reshape(block_len, heads_here * head_dim))
        key_total = key_total.at[:finish].add(key_part)
        value_total = value_total.at[:finish].add(value_part)
    key_list = key_total.astype(jnp.bfloat16).reshape(pack_len, kv_here * head_dim)
    value_list = value_total.astype(jnp.bfloat16).reshape(pack_len, kv_here * head_dim)
    inverse = jnp.zeros_like(order).at[order].set(jnp.arange(block_count, dtype=jnp.int32))

    def restore(rows):
        blocks = rows.reshape(block_count, -1, rows.shape[-1])
        return jnp.take(blocks, inverse, axis=0).reshape(group_rows, 1, rows.shape[-1])

    query_rows = restore(jnp.concatenate(query_list, axis=0))
    key_rows = restore(key_list)
    value_rows = restore(value_list)
    query_back, key_back, value_back = (
        lax.all_to_all(query_rows, "seq", split_axis=0, concat_axis=1, tiled=True),
        lax.all_to_all(key_rows, "seq", split_axis=0, concat_axis=1, tiled=True),
        lax.all_to_all(value_rows, "seq", split_axis=0, concat_axis=1, tiled=True),
    )
    key_grad = (
        key_back.reshape(tok_rows, KVH, repeat_factor, head_dim)
        .astype(jnp.float32)
        .sum(axis=2)
        .astype(jnp.bfloat16)
        .reshape(tok_rows, KVH * head_dim)
    )
    value_grad = (
        value_back.reshape(tok_rows, KVH, repeat_factor, head_dim)
        .astype(jnp.float32)
        .sum(axis=2)
        .astype(jnp.bfloat16)
        .reshape(tok_rows, KVH * head_dim)
    )
    query_grad = query_back.reshape(tok_rows, QH * head_dim)
    totals = jnp.concatenate(
        [
            jnp.sum(query_grad.astype(jnp.float32), axis=0),
            jnp.sum(value_grad.astype(jnp.float32), axis=0),
        ]
    )
    token_count = tok_rows * seq_count * lax.axis_size("fsdp")
    totals = totals / math.sqrt(token_count)
    summed = lax.psum(totals, "seq")
    bias_grads = lax.psum_scatter(summed, "fsdp", scatter_dimension=0, tiled=True)
    return (query_grad, key_grad, value_grad, bias_grads)


def solution(mesh):
    placed = (
        P(("fsdp", "seq"), None),
        P(("fsdp", "seq"), None),
        P(("fsdp", "seq"), None),
        P(("fsdp", "seq"), None),
        P("fsdp", None),
        P("fsdp", None, None),
    )
    return jax.shard_map(
        local,
        mesh=mesh,
        in_specs=placed,
        out_specs=(
            P(("fsdp", "seq"), None),
            P(("fsdp", "seq"), None),
            P(("fsdp", "seq"), None),
            P("fsdp"),
        ),
        check_vma=False,
    )
```

profile of v0, /device:TPU:1, one launch (start us, length us, event | category | flops | bytes accessed | tf_op | source)
XLA Modules:
  0.0 668.4 jit_solution(9909443917296166089)
XLA Ops:
  2.5 19.2 %all-to-all-start = ((bf16[128,16,128]{2,0,1:T(8,128)(2,1)}), bf16[128,16,128]{2,0,1:T(8,128)(2,1)S(1)}, u32[]{:S(2)}, u32[]{:S(2)}) async-start(bf16[128,16,128]{2,0,1:T(8,128)(2,1)} %bitcast.3), calls=%async_computation | async-start | bytes 1048576 | tf_op jit(solution)/shard_map/all_to_all | solution.py:62
  22.8 18.3 %all-to-all-done = bf16[128,16,128]{2,0,1:T(8,128)(2,1)S(1)} async-done(((bf16[128,16,128]{2,0,1:T(8,128)(2,1)}), bf16[128,16,128]{2,0,1:T(8,128)(2,1)S(1)}, u32[]{:S(2)}, u32[]{:S(2)}) %all-to-all-start) | async-done | bytes 524320 | tf_op jit(solution)/shard_map/all_to_all | solution.py:62
  42.0 4.2 all-to-all-start.2
  47.5 17.2 %all-to-all-done.2 = bf16[128,16,128]{2,0,1:T(8,128)(2,1)S(1)} async-done(((bf16[128,16,128]{2,0,1:T(8,128)(2,1)}), bf16[128,16,128]{2,0,1:T(8,128)(2,1)S(1)}, u32[]{:S(2)}, u32[]{:S(2)}) %all-to-all-start.2) | async-done | bytes 524320 | tf_op jit(solution)/shard_map/all_to_all | solution.py:63
  64.8 7.2 %all-to-all-start.1 = ((bf16[128,16,256]{0,2,1:T(8,128)(2,1)}), bf16[128,16,256]{0,2,1:T(8,128)(2,1)S(1)}, u32[]{:S(2)}, u32[]{:S(2)}) async-start(bf16[128,16,256]{0,2,1:T(8,128)(2,1)} %bitcast.12), calls=%async_computation.1 | async-start | bytes 2097152 | tf_op jit(solution)/shard_map/all_to_all | solution.py:61
  71.9 2.3 copy.175
  74.2 23.2 %all-to-all-done.1 = bf16[128,16,256]{0,2,1:T(8,128)(2,1)S(1)} async-done(((bf16[128,16,256]{0,2,1:T(8,128)(2,1)}), bf16[128,16,256]{0,2,1:T(8,128)(2,1)S(1)}, u32[]{:S(2)}, u32[]{:S(2)}) %all-to-all-start.1) | async-done | bytes 1048608 | tf_op jit(solution)/shard_map/all_to_all | solution.py:61
  97.5 11.0 %all-to-all-start.3 = ((bf16[128,16,256]{0,2,1:T(8,128)(2,1)}), bf16[128,16,256]{0,2,1:T(8,128)(2,1)}, u32[]{:S(2)}, u32[]{:S(2)}) async-start(bf16[128,16,256]{0,2,1:T(8,128)(2,1)} %bitcast.26), calls=%async_computation.3 | async-start | bytes 2097152 | tf_op jit(solution)/shard_map/all_to_all | solution.py:64
  112.4 1.8 fusion.13
  114.9 1.7 gather_fusion.2
  118.7 32.1 %all-to-all-done.3 = bf16[128,16,256]{0,2,1:T(8,128)(2,1)} async-done(((bf16[128,16,256]{0,2,1:T(8,128)(2,1)}), bf16[128,16,256]{0,2,1:T(8,128)(2,1)}, u32[]{:S(2)}, u32[]{:S(2)}) %all-to-all-start.3) | async-done | bytes 1048608 | tf_op jit(solution)/shard_map/all_to_all | solution.py:64
  150.8 2.3 copy.176
  153.1 1.8 gather_fusion.3
  154.9 1.6 broadcast_select_fusion.2
  167.0 4.8 fusion.8
  175.6 15.6 %fusion.4 = (f32[2,512]{1,0:T(2,128)S(1)}, bf16[1,2,512,1536]{2,3,1,0:T(8,128)(2,1)S(1)}, f32[1536,512,2]{1,0,2:T(8,128)}) fusion(f32[2,512]{1,0:T(2,128)S(1)} %fusion.6, f32[2,512]{1,0:T(2,128)S(1)} %get-tuple-element.159, f32[1536,512,2]{1,0,2:T(8,128)S(1)} %get-tuple-element.160, pred[512,1536]{0,1:T(8,128)(4,1)S(1)} %copy-done.15, ...), kind=kOutput, calls=%fused_computation.20 | convolution fusion | flops 415235072 | bytes 17182720 | tf_op jit(solution)/shard_map/qgrd,kgd->grqk/dot_general | solution.py:26
  193.5 2.2 fusion.3
  195.7 2.0 fusion.2
  197.7 5.4 fusion
  203.1 2.0 copy-done.4
  205.2 2.3 fusion.43
  207.5 2.1 copy.217
  209.5 3.1 fusion.48
  214.5 4.0 fusion.16
  220.7 4.9 fusion.10
  225.6 1.9 copy-done.2
  227.5 2.3 fusion.42
  229.8 2.0 copy.206
  231.8 2.5 gather_fusion.6
  234.3 2.5 gather_fusion.5
  236.7 2.3 broadcast_select_fusion.3
  239.6 2.7 reduce.36
  242.3 2.0 reshape.793
  244.3 4.6 all-to-all-start.5
  248.9 2.7 reduce.37
  251.6 2.0 reshape.795
  253.6 13.9 %all-to-all-done.5 = bf16[16,2,8192]{2,1,0:T(2,128)(2,1)} async-done(((bf16[16,2,8192]{2,1,0:T(2,128)(2,1)}), bf16[16,2,8192]{2,1,0:T(2,128)(2,1)}, u32[]{:S(2)}, u32[]{:S(2)}) %all-to-all-start.5) | async-done | bytes 524320 | tf_op jit(solution)/shard_map/all_to_all | solution.py:113
  267.5 5.1 all-to-all-start.6
  272.6 1.6 fusion.67
  275.1 2.2 fusion.68
  279.9 3.1 fusion.69
  286.6 8.2 %all-to-all-done.6 = bf16[16,2,8192]{2,1,0:T(2,128)(2,1)} async-done(((bf16[16,2,8192]{2,1,0:T(2,128)(2,1)}), bf16[16,2,8192]{2,1,0:T(2,128)(2,1)}, u32[]{:S(2)}, u32[]{:S(2)}) %all-to-all-start.6) | async-done | bytes 524320 | tf_op jit(solution)/shard_map/all_to_all | solution.py:114
  294.8 6.3 all-to-all-start.4
  303.0 2.2 reshape.796
  306.5 2.2 reshape.794
  310.0 15.6 %all-to-all-done.4 = bf16[16,2,16384]{2,1,0:T(2,128)(2,1)S(1)} async-done(((bf16[16,2,16384]{2,1,0:T(2,128)(2,1)}), bf16[16,2,16384]{2,1,0:T(2,128)(2,1)S(1)}, u32[]{:S(2)}, u32[]{:S(2)}) %all-to-all-start.4) | async-done | bytes 1048608 | tf_op jit(solution)/shard_map/all_to_all | solution.py:112
  329.0 248.6 %all-reduce.2 = f32[5120]{0:T(1024)S(1)} all-reduce(f32[5120]{0:T(1024)S(1)} %maximum_multiply_fusion), channel_id=2, replica_groups=mesh['fsdp'=32,'seq'=16] {'fsdp'}, use_global_device_ids=true, to_apply=%region_18.21.clone | all-reduce | flops 5120 | bytes 40960
  577.6 90.5 %psum.8 = f32[160]{0:T(256)} all-reduce(f32[160]{0:T(256)S(1)} %dynamic-slice.63), channel_id=1, replica_groups=mesh['fsdp'=32,'seq'=16] {'seq'}, use_global_device_ids=true, to_apply=%region_17.20 | all-reduce | flops 160 | bytes 1280 | tf_op jit(solution)/shard_map/psum | solution.py:139
  (137 shorter events, 46.8 us)
Async XLA Ops:
  0.6 1.0 copy-start
  0.6 45.6 %copy-start.18 = (bf16[128,4096]{1,0:T(8,128)(2,1)S(1)}, bf16[128,4096]{1,0:T(8,128)(2,1)}, u32[]{:S(2)}) copy-start(bf16[128,4096]{1,0:T(8,128)(2,1)} %param.30) | copy-start | bytes 3145732
  2.5 38.6 %all-to-all-start = ((bf16[128,16,128]{2,0,1:T(8,128)(2,1)}), bf16[128,16,128]{2,0,1:T(8,128)(2,1)S(1)}, u32[]{:S(2)}, u32[]{:S(2)}) async-start(bf16[128,16,128]{2,0,1:T(8,128)(2,1)} %bitcast.3), calls=%async_computation | async-start | bytes 1048576 | tf_op jit(solution)/shard_map/all_to_all | solution.py:62
  42.0 22.8 %all-to-all-start.2 = ((bf16[128,16,128]{2,0,1:T(8,128)(2,1)}), bf16[128,16,128]{2,0,1:T(8,128)(2,1)S(1)}, u32[]{:S(2)}, u32[]{:S(2)}) async-start(bf16[128,16,128]{2,0,1:T(8,128)(2,1)} %bitcast.19), calls=%async_computation.2 | async-start | bytes 1048576 | tf_op jit(solution)/shard_map/all_to_all | solution.py:63
  46.2 62.2 %copy-start.30 = (s32[1,64]{1,0:T(1,128)S(1)}, s32[1,64]{1,0:T(1,128)}, u32[]{:S(2)}) copy-start(s32[1,64]{1,0:T(1,128)} %param.34) | copy-start | bytes 772
  46.2 63.1 %copy-start.29 = (s32[1,1,2048]{2,1,0:T(1,128)S(1)}, s32[1,1,2048]{2,1,0:T(1,128)}, u32[]{:S(2)}) copy-start(s32[1,1,2048]{2,1,0:T(1,128)} %param.35) | copy-start | bytes 24580
  46.2 64.1 %slice-start = ((s32[1,1,2048]{2,1,0:T(1,128)}), s32[1,1,1024]{2,1,0:T(1,128)S(1)}, s32[]{:S(2)}) async-start(s32[1,1,2048]{2,1,0:T(1,128)} %param.35), calls=%async_computation.7 | async-start | bytes 8192 | tf_op jit(solution)/shard_map/slice | solution.py:93
  64.8 49.4 %copy-start.17 = (bf16[128,16,128]{2,0,1:T(8,128)(2,1)}, bf16[128,16,128]{2,0,1:T(8,128)(2,1)S(1)}, u32[]{:S(2)}) copy-start(bf16[128,16,128]{2,0,1:T(8,128)(2,1)S(1)} %all-to-all-done.2) | copy-start | bytes 1572868
  64.8 32.7 %all-to-all-start.1 = ((bf16[128,16,256]{0,2,1:T(8,128)(2,1)}), bf16[128,16,256]{0,2,1:T(8,128)(2,1)S(1)}, u32[]{:S(2)}, u32[]{:S(2)}) async-start(bf16[128,16,256]{0,2,1:T(8,128)(2,1)} %bitcast.12), calls=%async_computation.1 | async-start | bytes 2097152 | tf_op jit(solution)/shard_map/all_to_all | solution.py:61
  97.5 53.3 %all-to-all-start.3 = ((bf16[128,16,256]{0,2,1:T(8,128)(2,1)}), bf16[128,16,256]{0,2,1:T(8,128)(2,1)}, u32[]{:S(2)}, u32[]{:S(2)}) async-start(bf16[128,16,256]{0,2,1:T(8,128)(2,1)} %bitcast.26), calls=%async_computation.3 | async-start | bytes 2097152 | tf_op jit(solution)/shard_map/all_to_all | solution.py:64
  110.8 55.2 %copy-start.16 = (pred[512,1024]{0,1:T(8,128)(4,1)}, pred[512,1024]{0,1:T(8,128)(4,1)S(1)}, u32[]{:S(2)}) copy-start(pred[512,1024]{0,1:T(8,128)(4,1)S(1)} %fusion.51) | copy-start | bytes 1572868
  117.5 47.5 %copy-start.11 = (bf16[64,32,128]{2,1,0:T(8,128)(2,1)}, bf16[64,32,128]{2,1,0:T(8,128)(2,1)S(1)}, u32[]{:S(2)}) copy-start(bf16[64,32,128]{2,1,0:T(8,128)(2,1)S(1)} %get-tuple-element.155) | copy-start | bytes 1572868
  156.6 2.9 copy-start.13
  159.5 3.2 copy-start.24
  160.2 2.6 copy-start.28
  163.3 1.0 copy-start.25
  163.8 1.2 copy-start.26
  164.3 1.7 copy-start.10
  167.0 5.6 copy-start.12
  167.0 5.6 copy-start.15
  167.0 5.6 copy-start.20
  191.2 4.5 copy-start.6
  191.2 2.0 copy-start.14
  191.2 2.2 copy-start.19
  203.1 2.0 copy-start.4
  209.5 3.1 copy-start.27
  209.5 4.9 copy-start.7
  212.6 1.3 copy-start.3
  213.5 1.0 copy-start.8
  214.5 4.0 copy-start.9
  214.5 4.0 copy-start.21
  218.5 2.2 copy-start.5
  225.5 1.9 copy-start.2
  244.3 23.2 %all-to-all-start.5 = ((bf16[16,2,8192]{2,1,0:T(2,128)(2,1)}), bf16[16,2,8192]{2,1,0:T(2,128)(2,1)}, u32[]{:S(2)}, u32[]{:S(2)}) async-start(bf16[16,2,8192]{2,1,0:T(2,128)(2,1)} %reshape.793), calls=%async_computation.5 | async-start | bytes 1048576 | tf_op jit(solution)/shard_map/all_to_all | solution.py:113
  267.5 27.3 %all-to-all-start.6 = ((bf16[16,2,8192]{2,1,0:T(2,128)(2,1)}), bf16[16,2,8192]{2,1,0:T(2,128)(2,1)}, u32[]{:S(2)}, u32[]{:S(2)}) async-start(bf16[16,2,8192]{2,1,0:T(2,128)(2,1)} %reshape.795), calls=%async_computation.6 | async-start | bytes 1048576 | tf_op jit(solution)/shard_map/all_to_all | solution.py:114
  279.7 3.4 copy-start.22
  279.7 3.4 copy-start.23
  294.8 30.8 %all-to-all-start.4 = ((bf16[16,2,16384]{2,1,0:T(2,128)(2,1)}), bf16[16,2,16384]{2,1,0:T(2,128)(2,1)S(1)}, u32[]{:S(2)}, u32[]{:S(2)}) async-start(bf16[16,2,16384]{2,1,0:T(2,128)(2,1)} %reshape.791), calls=%async_computation.4 | async-start | bytes 2097152 | tf_op jit(solution)/shard_map/all_to_all | solution.py:112
  325.6 342.6 %copy-start.1 = (bf16[128,1024]{1,0:T(8,128)(2,1)S(1)}, bf16[128,1024]{1,0:T(8,128)(2,1)}, u32[]{:S(2)}) copy-start(bf16[128,1024]{1,0:T(8,128)(2,1)} %param.31) | copy-start | bytes 786436
where the time goes:
time: 675 us; the launch traced here: 668 us
  blocking collectives  339 us (50%)
  waiting for transfers between devices  129 us (19%)
  starting transfers between devices  57.6 us (9%)
  local copies, waits for them, and re-layouts  55.6 us (8%)
  matrix products  50.7 us (8%)
  other arithmetic  34.6 us (5%)
    unnamed x1, blocking collectives  249 us
    psum x1, blocking collectives, local(): summed = lax.psum(totals, 'seq')  90.5 us
    all_to_all x1, waiting for transfers between devices, local(): lax.all_to_all(grad_split, 'seq', split_axis=1, concat_axis=0, tiled=True)  32.1 us
    unnamed x79, local copies, waits for them, and re-layouts  26.8 us
    dot_general x4, matrix products, block_gradients(): jnp.einsum('qgrd,kgd->grqk', grad_block, value_range, preferred_element_t...  26.4 us
    all_to_all x1, waiting for transfers between devices, local(): lax.all_to_all(query_split, 'seq', split_axis=1, concat_axis=0, tiled=True)  23.2 us
    all_to_all x1, starting transfers between devices, local(): lax.all_to_all(key_slots, 'seq', split_axis=1, concat_axis=0, tiled=True)  19.2 us
    all_to_all x1, waiting for transfers between devices, local(): lax.all_to_all(key_slots, 'seq', split_axis=1, concat_axis=0, tiled=True)  18.3 us
  transfers between devices with their start and end apart: 7, of which 7 were waited for; matrix products, arithmetic and copies ran while one was open for 6% of the time, Pallas kernels for 0%

commit v1 on v0

v1 whole, which is shorter than its diff:
```python
import math

import jax
import jax.numpy as jnp
from jax import lax
from jax.experimental import pallas as pl
from jax.experimental.pallas import tpu as pltpu
from jax.sharding import PartitionSpec as P

QH = 32
KVH = 8
HD = 128
TOK = 128
HALF = 1024
FULL = 2048
GROUP = 4
GCOL = GROUP * HD
COLS = GROUP * HALF
TILE = 256
NX = 4
NZ = 8
BIG = 1e30
MESH = pl.DeviceIdType.MESH
F32 = jnp.float32
BF16 = jnp.bfloat16


def dot(a, b):
    return jnp.dot(a, b, preferred_element_type=F32)


def dot_nt(a, b):
    return lax.dot_general(a, b, (((1,), (1,)), ((), ())), preferred_element_type=F32)


def at128(index):
    return pl.multiple_of(index, 128)


def kernel(
    q_ref, k_ref, v_ref, g_ref, order_ref, docs_ref,
    dq_out, dk_out, dv_out, bias_out,
    qbuf, gbuf, kbuf, vbuf, km, qm, ordpad, sbuf, ebuf, gs, invl, kt, vt,
    dqb, dkb, dvb, dkl, dvl, b0, b1, b2, bl1, bl2, bl3,
    q_ss, q_rs, g_ss, g_rs, k_ss, k_rs, v_ss, v_rs,
    dq_ss, dq_rs, dk_ss, dk_rs, dv_ss, dv_rs,
    z_ss, z_rs, x_ss, x_rs, h_ss, h_rs, own_sem,
):
    f = lax.axis_index("fsdp")
    s = lax.axis_index("seq")
    x = lax.rem(f, NX)
    zl = f // NX
    y = s // 4
    zh = lax.rem(s // 2, 2)
    c = lax.rem(s, 2)
    me = y * 2 + c
    zi = zh * NZ + zl
    scaling = 1.0 / math.sqrt(HD)

    def seq_of(slot, half):
        return (slot // 2) * 4 + half * 2 + lax.rem(slot, 2)

    def remote(src, dst, ss, rs, fs, sq):
        return pltpu.make_async_remote_copy(
            src_ref=src, dst_ref=dst, send_sem=ss, recv_sem=rs,
            device_id={"fsdp": fs, "seq": sq}, device_id_type=MESH,
        )

    def repeat(low, high, body):
        def step(i, carry):
            body(i)
            return carry

        lax.fori_loop(low, high, step, 0)

    def other_slot(d):
        return lax.rem(y + d // 2, 4) * 2 + lax.rem(c + d, 2)

    def own_slot(d):
        return lax.rem(me + d, 8)

    barrier = pltpu.get_barrier_semaphore()

    def greet(fs, sq):
        pl.semaphore_signal(
            barrier, inc=1, device_id={"fsdp": fs, "seq": sq}, device_id_type=MESH
        )

    repeat(1, 16, lambda d: greet(f, lax.rem(s + d, 16)))

    def greet_line(d):
        there = lax.rem(zl + d, NZ) * NX + x
        greet(there, s)
        greet(there, seq_of(me, 1 - zh))

    repeat(1, NZ, greet_line)
    repeat(1, NX, lambda d: greet(zl * NX + lax.rem(x + d, NX), s))

    def own_copies():
        rows = pl.ds(at128(me * TOK), TOK)
        wide = pl.ds(at128(me * GCOL), GCOL)
        thin = pl.ds(at128(me * HD), HD)
        return [
            pltpu.make_async_copy(k_ref.at[:, thin], kbuf.at[rows], own_sem.at[0]),
            pltpu.make_async_copy(q_ref.at[:, wide], qbuf.at[rows], own_sem.at[1]),
            pltpu.make_async_copy(g_ref.at[:, wide], gbuf.at[rows], own_sem.at[2]),
            pltpu.make_async_copy(v_ref.at[:, thin], vbuf.at[rows], own_sem.at[3]),
        ]

    for copy in own_copies():
        copy.start()
    pl.semaphore_wait(barrier, 15 + 2 * (NZ - 1) + (NX - 1))

    def narrow_copy(src, dst, ss, rs, slot, away, sender):
        return remote(
            src.at[:, pl.ds(at128(slot * HD), HD)],
            dst.at[pl.ds(at128(away * HALF + sender * TOK), TOK)],
            ss.at[away * 8 + slot],
            rs.at[away * 8 + sender],
            f,
            seq_of(slot, zh ^ away),
        )

    def wide_copy(src, dst, ss, rs, slot, sender):
        return remote(
            src.at[:, pl.ds(at128(slot * GCOL), GCOL)],
            dst.at[pl.ds(at128(sender * TOK), TOK)],
            ss.at[slot],
            rs.at[sender],
            f,
            seq_of(slot, zh),
        )

    def k_copy(slot, away, sender):
        return narrow_copy(k_ref, kbuf, k_ss, k_rs, slot, away, sender)

    def v_copy(slot, away, sender):
        return narrow_copy(v_ref, vbuf, v_ss, v_rs, slot, away, sender)

    def q_copy(slot, sender):
        return wide_copy(q_ref, qbuf, q_ss, q_rs, slot, sender)

    def g_copy(slot, sender):
        return wide_copy(g_ref, gbuf, g_ss, g_rs, slot, sender)

    repeat(0, 8, lambda d: k_copy(other_slot(d), 1, me).start())
    repeat(1, 8, lambda d: k_copy(own_slot(d), 0, me).start())
    repeat(1, 8, lambda d: q_copy(own_slot(d), me).start())
    repeat(1, 8, lambda d: g_copy(own_slot(d), me).start())
    repeat(1, 8, lambda d: v_copy(own_slot(d), 0, me).start())

    ordpad[...] = jnp.full((8, 128), -1, jnp.int32)
    ordpad[0:1, 0:64] = order_ref[...]
    docs = docs_ref[...]
    starts = [
        jnp.sum(jnp.where(docs < d, 1.0, 0.0).astype(F32), axis=1, keepdims=True)
        for d in (1, 2, 3)
    ]

    def mask_columns(chunk):
        base = pl.multiple_of(chunk * TILE, TILE)
        row = lax.broadcasted_iota(jnp.int32, (TILE, 128), 0) + base
        lane = lax.broadcasted_iota(jnp.int32, (TILE, 128), 1)
        half = (row >> 10) ^ zh
        slot = (row >> 7) & 7
        block = (((slot >> 1) * 4 + half * 2 + (slot & 1)) << 2) + ((row >> 5) & 3)
        hot = ordpad[0:1, :] == block
        lanes = lane.astype(F32)
        place = jnp.sum(jnp.where(hot, lanes, 0.0), axis=1, keepdims=True)
        pos = place * 32.0 + (row[:, 0:1] & 31).astype(F32)
        doc = jnp.zeros((TILE, 1), F32)
        for start in starts:
            doc = doc + jnp.where(pos >= start, 1.0, 0.0)
        same = (lanes - 64.0) == doc
        first = lane < 64
        km[pl.ds(base, TILE), :] = jnp.where(
            first, jnp.where(hot, 1.0, 0.0), jnp.where(same, 1.0, 0.0)
        ).astype(BF16)

        later = jnp.where(lanes > place, -BIG, 0.0)
        differs = jnp.where(same | (lane >= 68), 0.0, -BIG)
        return jnp.where(first, later, differs).astype(BF16)

    def own_mask(chunk):
        qm[pl.ds(pl.multiple_of(chunk * TILE, TILE), TILE), :] = mask_columns(chunk)

    def other_mask(chunk):
        mask_columns(chunk)

    repeat(0, 4, own_mask)
    repeat(4, 8, other_mask)

    repeat(0, 8, lambda d: k_copy(other_slot(d), 1, me).wait_send())
    repeat(0, 8, lambda d: v_copy(other_slot(d), 1, me).start())

    own = own_copies()
    own[0].wait()
    own[1].wait()
    repeat(1, 8, lambda d: q_copy(me, own_slot(d)).wait_recv())
    repeat(1, 8, lambda d: k_copy(me, 0, own_slot(d)).wait_recv())
    repeat(0, 8, lambda d: k_copy(me, 1, other_slot(d)).wait_recv())

    tri_row = lax.broadcasted_iota(jnp.int32, (TILE, TILE), 0)
    tri_col = lax.broadcasted_iota(jnp.int32, (TILE, TILE), 1)
    triangle = jnp.where(
        ((tri_row >> 5) == (tri_col >> 5)) & (tri_row > tri_col), -BIG, 0.0
    ).astype(F32)
    nq = HALF // TILE
    nk = FULL // TILE
    exponent_scale = scaling * math.log2(math.e)

    def head_scores(head):
        lanes = pl.ds(at128(head * HD), HD)

        def query_tile(qt):
            rows = slice(qt * TILE, (qt + 1) * TILE)
            return jnp.concatenate([qbuf[rows, lanes], qm[rows, :]], axis=1)

        def score_chunk(qt, kc, q_tile, top):
            rows = slice(kc * TILE, (kc + 1) * TILE)
            k_tile = jnp.concatenate([kbuf[rows, :], km[rows, :]], axis=1)
            scores = dot_nt(k_tile, q_tile)
            if kc == qt:
                scores = scores + triangle
            sbuf[qt % 2, rows, :] = scores
            part = jnp.max(scores.reshape(TILE // 8, 8, TILE), axis=0)
            return part if top is None else jnp.maximum(top, part)

        def exp_chunk(qt, kc, top, total):
            rows = slice(kc * TILE, (kc + 1) * TILE)
            cols = pl.ds(at128(head * HALF + qt * TILE), TILE)
            exponent = jnp.exp2((sbuf[qt % 2, rows, :] - top) * exponent_scale)
            ebuf[rows, cols] = exponent.astype(BF16)
            part = jnp.sum(exponent.reshape(TILE // 8, 8, TILE), axis=0)
            return part if total is None else total + part

        tops = [None] * nq
        q_tile = query_tile(0)
        for kc in range(nk):
            tops[0] = score_chunk(0, kc, q_tile, tops[0])
        for qt in range(nq):
            top = jnp.max(tops[qt], axis=0, keepdims=True)
            total = None
            if qt + 1 < nq:
                q_tile = query_tile(qt + 1)
            for kc in range(nk):
                if qt + 1 < nq:
                    tops[qt + 1] = score_chunk(qt + 1, kc, q_tile, tops[qt + 1])
                total = exp_chunk(qt, kc, top, total)
            cols = pl.ds(at128(head * HALF + qt * TILE), TILE)
            invl[0:1, cols] = 1.0 / jnp.sum(total, axis=0, keepdims=True)

    repeat(0, GROUP, head_scores)

    own[2].wait()
    repeat(1, 8, lambda d: g_copy(me, own_slot(d)).wait_recv())

    def scale_cotangents(head):
        for qt in range(nq):
            cols = pl.ds(at128(head * HALF + qt * TILE), TILE)
            inverse = jnp.broadcast_to(invl[0:1, cols], (HD, TILE)).T
            piece = gbuf[qt * TILE : (qt + 1) * TILE, pl.ds(at128(head * HD), HD)]
            gs[cols, 0:HD] = (piece.astype(F32) * inverse).astype(BF16)

    repeat(0, GROUP, scale_cotangents)

    def back_copy(src, dst, ss, rs, slot, away, sender):
        return remote(
            src.at[pl.ds(at128(away * HALF + slot * TOK), TOK)],
            dst.at[away, sender],
            ss.at[away * 8 + slot],
            rs.at[away * 8 + sender],
            f,
            seq_of(slot, zh ^ away),
        )

    def dv_copy(slot, away, sender):
        return back_copy(dvb, dvl, dv_ss, dv_rs, slot, away, sender)

    def dk_copy(slot, away, sender):
        return back_copy(dkb, dkl, dk_ss, dk_rs, slot, away, sender)

    def value_chunk(row, sums):
        rows = pl.ds(pl.multiple_of(row, TILE), TILE)
        acc = jnp.zeros((TILE, HD), F32)
        for head in range(GROUP):
            span = slice(head * HALF, (head + 1) * HALF)
            acc = acc + dot(ebuf[rows, span], gs[span, 0:HD])
        dvb[rows, :] = acc.astype(BF16)
        return sums + jnp.sum(acc.reshape(TILE // 8, 8, HD), axis=0)

    def value_other(i, sums):
        column = lax.rem(y + i, 4)
        sums = value_chunk(HALF + column * TILE, sums)
        dv_copy(column * 2, 1, me).start()
        dv_copy(column * 2 + 1, 1, me).start()
        return sums

    sums = lax.fori_loop(0, 4, value_other, jnp.zeros((8, HD), F32))
    sums = lax.fori_loop(0, 4, lambda i, carry: value_chunk(i * TILE, carry), sums)
    repeat(1, 8, lambda d: dv_copy(own_slot(d), 0, me).start())
    b0[...] = jnp.zeros((8, 128), F32)
    b0[4:5, :] = jnp.sum(sums, axis=0, keepdims=True)

    own[3].wait()
    repeat(1, 8, lambda d: v_copy(me, 0, own_slot(d)).wait_recv())
    repeat(0, 8, lambda d: v_copy(me, 1, other_slot(d)).wait_recv())
    for chunk in range(nk):
        rows = slice(chunk * TILE, (chunk + 1) * TILE)
        vt[:, rows] = vbuf[rows, :].T
        kt[:, rows] = kbuf[rows, :].T

    lane = lax.broadcasted_iota(jnp.int32, (TILE, 128), 1)

    def row_dots(head):
        for qt in range(nq):
            cols = pl.ds(at128(head * HALF + qt * TILE), TILE)
            mixed = dot(vt[...], ebuf[:, cols]) * invl[0:1, cols]
            row_dot = jnp.sum(gs[cols, 0:HD].astype(F32) * mixed.T, axis=1, keepdims=True)
            high = row_dot.astype(BF16).astype(F32)
            rest = row_dot - high
            mid = rest.astype(BF16).astype(F32)
            low = rest - mid
            pieces = jnp.where(
                lane == 0, high, jnp.where(lane == 1, mid, jnp.where(lane == 2, low, 0.0))
            )
            gs[cols, HD : 2 * HD] = (-pieces).astype(BF16)

    repeat(0, GROUP, row_dots)

    ones = jnp.where(lane < 3, 1.0, 0.0).astype(BF16)

    def key_chunk(row):
        rows = pl.ds(pl.multiple_of(row, TILE), TILE)
        v_tile = jnp.concatenate([vbuf[rows, :], ones], axis=1)
        acc = jnp.zeros((TILE, HD), F32)
        for head in range(GROUP):
            span = slice(head * HALF, (head + 1) * HALF)
            centred = dot_nt(v_tile, gs[span, :])
            grad = centred.astype(BF16) * ebuf[rows, span]
            ebuf[rows, span] = grad
            acc = acc + dot(grad, qbuf[:, head * HD : (head + 1) * HD])
        dkb[rows, :] = (acc * scaling).astype(BF16)

    def key_other(i):
        column = lax.rem(y + i, 4)
        key_chunk(HALF + column * TILE)
        dk_copy(column * 2, 1, me).start()
        dk_copy(column * 2 + 1, 1, me).start()

    repeat(0, 4, key_other)
    repeat(0, 4, lambda i: key_chunk(i * TILE))
    repeat(1, 8, lambda d: dk_copy(own_slot(d), 0, me).start())

    def query_rows(qt, sums):
        sums = list(sums)
        for head in range(GROUP):
            cols = pl.ds(at128(head * HALF + qt * TILE), TILE)
            piece = ((dot(kt[...], ebuf[:, cols]) * scaling).T).astype(BF16)
            dqb[pl.ds(pl.multiple_of(qt * TILE, TILE), TILE), head * HD : (head + 1) * HD] = piece
            wide = piece.astype(F32).reshape(TILE // 8, 8, HD)
            sums[head] = sums[head] + jnp.sum(wide, axis=0)
        return tuple(sums)

    zero = jnp.zeros((8, HD), F32)
    q_sums = lax.fori_loop(0, nq, query_rows, (zero,) * GROUP)
    for head in range(GROUP):
        b0[head : head + 1, :] = jnp.sum(q_sums[head], axis=0, keepdims=True)

    def z_copy(d, far, target):
        there = lax.rem(zl + d, NZ)
        return remote(
            b0, bl1.at[target], z_ss.at[far * NZ + d], z_rs.at[target],
            there * NX + x, seq_of(me, zh ^ far),
        )

    def z_from(d, far):
        return z_copy(d, far, (zh ^ far) * NZ + lax.rem(zl + d, NZ))

    repeat(1, NZ, lambda d: z_copy(d, 0, zi).start())
    repeat(0, NZ, lambda d: z_copy(d, 1, zi).start())

    def dq_copy(slot, sender):
        return remote(
            dqb.at[pl.ds(at128(slot * TOK), TOK)],
            dq_out.at[:, pl.ds(at128(sender * GCOL), GCOL)],
            dq_ss.at[slot], dq_rs.at[sender], f, seq_of(slot, zh),
        )

    repeat(1, 8, lambda d: dq_copy(own_slot(d), me).start())
    own_dq = pltpu.make_async_copy(
        dqb.at[pl.ds(at128(me * TOK), TOK)],
        dq_out.at[:, pl.ds(at128(me * GCOL), GCOL)],
        own_sem.at[4],
    )
    own_dq.start()

    bl1[zi] = b0[...]
    repeat(1, NZ, lambda d: z_from(d, 0).wait_recv())
    repeat(0, NZ, lambda d: z_from(d, 1).wait_recv())
    b1[...] = jnp.sum(bl1[...], axis=0)

    def x_copy(d, target):
        return remote(
            b1, bl2.at[target], x_ss.at[d], x_rs.at[target],
            zl * NX + lax.rem(x + d, NX), s,
        )

    repeat(1, NX, lambda d: x_copy(d, x).start())
    bl2[x] = b1[...]
    repeat(1, NX, lambda d: x_copy(d, lax.rem(x + d, NX)).wait_recv())
    b2[...] = jnp.sum(bl2[...], axis=0) * (1.0 / 256.0)

    def h_copy(slot, sender):
        return remote(
            b2, bl3.at[sender], h_ss.at[slot], h_rs.at[sender], f, seq_of(slot, zh)
        )

    repeat(1, 8, lambda d: h_copy(own_slot(d), me).start())
    bl3[me] = b2[...]
    repeat(1, 8, lambda d: h_copy(me, own_slot(d)).wait_recv())
    for slot in range(8):
        bias_out[slot * 4 : slot * 4 + 4, :] = bl3[slot, 0:4, :]
        bias_out[32 + slot : 33 + slot, :] = bl3[slot, 4:5, :]

    def finish(buf, landed, copy_of, out):
        landed[0, me] = buf[pl.ds(at128(me * TOK), TOK), :]
        repeat(1, 8, lambda d: copy_of(me, 0, own_slot(d)).wait_recv())
        repeat(0, 8, lambda d: copy_of(me, 1, other_slot(d)).wait_recv())
        for slot in range(8):
            total = landed[0, slot].astype(F32) + landed[1, slot].astype(F32)
            out[:, slot * HD : (slot + 1) * HD] = total.astype(BF16)

    finish(dvb, dvl, dv_copy, dv_out)
    finish(dkb, dkl, dk_copy, dk_out)
    own_dq.wait()
    repeat(1, 8, lambda d: dq_copy(me, own_slot(d)).wait_recv())

    def near(d):
        slot = own_slot(d)
        k_copy(slot, 0, me).wait_send()
        v_copy(slot, 0, me).wait_send()
        q_copy(slot, me).wait_send()
        g_copy(slot, me).wait_send()
        dv_copy(slot, 0, me).wait_send()
        dk_copy(slot, 0, me).wait_send()
        dq_copy(slot, me).wait_send()
        h_copy(slot, me).wait_send()
        z_copy(d, 0, zi).wait_send()

    def far(d):
        slot = other_slot(d)
        v_copy(slot, 1, me).wait_send()
        dv_copy(slot, 1, me).wait_send()
        dk_copy(slot, 1, me).wait_send()
        z_copy(d, 1, zi).wait_send()

    repeat(1, 8, near)
    repeat(0, 8, far)
    repeat(1, NX, lambda d: x_copy(d, x).wait_send())


def local(query, key, value, out_grad, pack_order, doc_ids):
    vmem = pl.BlockSpec(memory_space=pltpu.VMEM)
    hbm = pl.BlockSpec(memory_space=pl.ANY)
    dma = pltpu.SemaphoreType.DMA
    query_grad, key_grad, value_grad, bias = pl.pallas_call(
        kernel,
        out_shape=(
            jax.ShapeDtypeStruct((TOK, QH * HD), BF16),
            jax.ShapeDtypeStruct((TOK, KVH * HD), BF16),
            jax.ShapeDtypeStruct((TOK, KVH * HD), BF16),
            jax.ShapeDtypeStruct((QH + KVH, HD), F32),
        ),
        in_specs=[hbm, hbm, hbm, hbm, vmem, vmem],
        out_specs=(hbm, vmem, vmem, vmem),
        scratch_shapes=[
            pltpu.VMEM((HALF, GCOL), BF16),
            pltpu.VMEM((HALF, GCOL), BF16),
            pltpu.VMEM((FULL, HD), BF16),
            pltpu.VMEM((FULL, HD), BF16),
            pltpu.VMEM((FULL, HD), BF16),
            pltpu.VMEM((HALF, HD), BF16),
            pltpu.VMEM((8, 128), jnp.int32),
            pltpu.VMEM((2, FULL, TILE), F32),
            pltpu.VMEM((FULL, COLS), BF16),
            pltpu.VMEM((COLS, 2 * HD), BF16),
            pltpu.VMEM((8, COLS), F32),
            pltpu.VMEM((HD, FULL), BF16),
            pltpu.VMEM((HD, FULL), BF16),
            pltpu.VMEM((HALF, GCOL), BF16),
            pltpu.VMEM((FULL, HD), BF16),
            pltpu.VMEM((FULL, HD), BF16),
            pltpu.VMEM((2, 8, TOK, HD), BF16),
            pltpu.VMEM((2, 8, TOK, HD), BF16),
            pltpu.VMEM((8, 128), F32),
            pltpu.VMEM((8, 128), F32),
            pltpu.VMEM((8, 128), F32),
            pltpu.VMEM((2 * NZ, 8, 128), F32),
            pltpu.VMEM((NX, 8, 128), F32),
            pltpu.VMEM((8, 8, 128), F32),
            dma((8,)), dma((8,)), dma((8,)), dma((8,)),
            dma((16,)), dma((16,)), dma((16,)), dma((16,)),
            dma((8,)), dma((8,)), dma((16,)), dma((16,)), dma((16,)), dma((16,)),
            dma((2 * NZ,)), dma((2 * NZ,)), dma((NX,)), dma((NX,)), dma((8,)), dma((8,)),
            dma((5,)),
        ],
        compiler_params=pltpu.CompilerParams(
            collective_id=0, has_side_effects=True, vmem_limit_bytes=56 << 20
        ),
        cost_estimate=pl.CostEstimate(
            flops=6 * 2 * COLS * FULL * HD, bytes_accessed=8 << 20, transcendentals=COLS * FULL
        ),
        name="attention_backward",
    )(query, key, value, out_grad, pack_order, doc_ids.reshape(1, FULL))
    width = (QH + KVH) * HD // lax.axis_size("fsdp")
    bias_grads = lax.dynamic_slice(
        bias.reshape((QH + KVH) * HD), (lax.axis_index("fsdp") * width,), (width,)
    )
    return (query_grad, key_grad, value_grad, bias_grads)


def solution(mesh):
    rows = P(("fsdp", "seq"), None)
    return jax.shard_map(
        local,
        mesh=mesh,
        in_specs=(rows, rows, rows, rows, P("fsdp", None), P("fsdp", None, None)),
        out_specs=(rows, rows, rows, P("fsdp")),
        check_vma=False,
    )
```

time: 675 us -> 141 us (0.21)
  the two profiles are of different devices: /device:TPU:1 before, /device:TPU:9 now
where the time goes in v1:
time: 141 us; the launch traced here: 140 us
  Pallas kernels  134 us (95%)
  local copies, waits for them, and re-layouts  5.42 us (4%)
    pallas_call x1, Pallas kernels, local(): pl.pallas_call(kernel, out_shape=(jax.ShapeDtypeStruct((TOK, QH * HD), BF...  134 us
    unnamed x7, local copies, waits for them, and re-layouts  4.08 us

profile of v1, /device:TPU:9, one launch (start us, length us, event | category | flops | bytes accessed | tf_op | source)
XLA Modules:
  0.0 140.3 jit_solution(9229118202728420009)
XLA Ops:
  0.6 134.3 %attention_backward.1 = (bf16[128,4096]{1,0:T(8,128)(2,1)}, bf16[128,1024]{1,0:T(8,128)(2,1)}, bf16[128,1024]{1,0:T(8,128)(2,1)}, f32[40,128]{1,0:T(8,128)}) custom-call(bf16[128,4096]{1,0:T(8,128)(2,1)} %q_ref.1, bf16[128,1024]{1,0:T(8,128)(2,1)} %k_ref.1, bf16[128,1024]{1,0:T(8,128)(2,1)} %v_ref.1, bf16[128,4096]{1,0:T(8,128)(2,1)} %g_ref.1, ...), custom_call_target="tpu_custom_call" | custom-call | flops 12884901888 | bytes 8388608 | tf_op jit(solution)/shard_map/attention_backward/pallas_call | solution.py:467
  134.9 1.3 dynamic_slice.3
  136.3 0.0 copy-start.1
  136.3 2.3 %copy.13 = bf16[128,4096]{1,0:T(8,128)(2,1)} copy(bf16[128,4096]{1,0:T(8,128)(2,1)} %get-tuple-element.16) | data formatting | bytes 2097152
  138.6 0.0 copy-done.1
  138.6 0.0 copy-start
  138.6 0.7 copy.14
  139.3 0.3 copy-done
  139.6 0.7 copy.15
Async XLA Ops:
  136.3 2.3 %copy-start.1 = (bf16[128,1024]{1,0:T(8,128)(2,1)S(1)}, bf16[128,1024]{1,0:T(8,128)(2,1)}, u32[]{:S(2)}) copy-start(bf16[128,1024]{1,0:T(8,128)(2,1)} %get-tuple-element.17) | copy-start | bytes 786436
  138.6 1.0 copy-start

commit v2 on v1

--- a/solution.py
+++ b/solution.py
@@ -19,6 +19,7 @@
 TILE = 256
 NX = 4
 NZ = 8
+WIDTH = (QH + KVH) * HD // (NX * NZ)
 BIG = 1e30
 MESH = pl.DeviceIdType.MESH
 F32 = jnp.float32
@@ -41,7 +42,7 @@
     q_ref, k_ref, v_ref, g_ref, order_ref, docs_ref,
     dq_out, dk_out, dv_out, bias_out,
     qbuf, gbuf, kbuf, vbuf, km, qm, ordpad, sbuf, ebuf, gs, invl, kt, vt,
-    dqb, dkb, dvb, dkl, dvl, b0, b1, b2, bl1, bl2, bl3,
+    dqb, dkb, dvb, dkl, dvl, b0, b1, brow, bl1, bl2, bl3,
     q_ss, q_rs, g_ss, g_rs, k_ss, k_rs, v_ss, v_rs,
     dq_ss, dq_rs, dk_ss, dk_rs, dv_ss, dv_rs,
     z_ss, z_rs, x_ss, x_rs, h_ss, h_rs, own_sem,
@@ -146,8 +147,6 @@
     repeat(0, 8, lambda d: k_copy(other_slot(d), 1, me).start())
     repeat(1, 8, lambda d: k_copy(own_slot(d), 0, me).start())
     repeat(1, 8, lambda d: q_copy(own_slot(d), me).start())
-    repeat(1, 8, lambda d: g_copy(own_slot(d), me).start())
-    repeat(1, 8, lambda d: v_copy(own_slot(d), 0, me).start())
 
     ordpad[...] = jnp.full((8, 128), -1, jnp.int32)
     ordpad[0:1, 0:64] = order_ref[...]
@@ -190,8 +189,13 @@
     repeat(0, 4, own_mask)
     repeat(4, 8, other_mask)
 
-    repeat(0, 8, lambda d: k_copy(other_slot(d), 1, me).wait_send())
-    repeat(0, 8, lambda d: v_copy(other_slot(d), 1, me).start())
+    def value_send(d):
+        k_copy(other_slot(d), 1, me).wait_send()
+        v_copy(other_slot(d), 1, me).start()
+
+    repeat(0, 8, value_send)
+    repeat(1, 8, lambda d: g_copy(own_slot(d), me).start())
+    repeat(1, 8, lambda d: v_copy(own_slot(d), 0, me).start())
 
     own = own_copies()
     own[0].wait()
@@ -330,27 +334,15 @@
 
     ones = jnp.where(lane < 3, 1.0, 0.0).astype(BF16)
 
-    def key_chunk(row):
-        rows = pl.ds(pl.multiple_of(row, TILE), TILE)
+    def score_gradients(i):
+        rows = pl.ds(pl.multiple_of(i * TILE, TILE), TILE)
         v_tile = jnp.concatenate([vbuf[rows, :], ones], axis=1)
-        acc = jnp.zeros((TILE, HD), F32)
         for head in range(GROUP):
             span = slice(head * HALF, (head + 1) * HALF)
             centred = dot_nt(v_tile, gs[span, :])
-            grad = centred.astype(BF16) * ebuf[rows, span]
-            ebuf[rows, span] = grad
-            acc = acc + dot(grad, qbuf[:, head * HD : (head + 1) * HD])
-        dkb[rows, :] = (acc * scaling).astype(BF16)
-
-    def key_other(i):
-        column = lax.rem(y + i, 4)
-        key_chunk(HALF + column * TILE)
-        dk_copy(column * 2, 1, me).start()
-        dk_copy(column * 2 + 1, 1, me).start()
-
-    repeat(0, 4, key_other)
-    repeat(0, 4, lambda i: key_chunk(i * TILE))
-    repeat(1, 8, lambda d: dk_copy(own_slot(d), 0, me).start())
+            ebuf[rows, span] = centred.astype(BF16) * ebuf[rows, span]
+
+    repeat(0, nk, score_gradients)
 
     def query_rows(qt, sums):
         sums = list(sums)
@@ -367,18 +359,58 @@
     for head in range(GROUP):
         b0[head : head + 1, :] = jnp.sum(q_sums[head], axis=0, keepdims=True)
 
+    def x_copy(d, target):
+        return remote(
+            b0, bl1.at[target], x_ss.at[d], x_rs.at[target],
+            zl * NX + lax.rem(x + d, NX), s,
+        )
+
+    repeat(1, NX, lambda d: x_copy(d, x).start())
+    bl1[x] = b0[...]
+    repeat(1, NX, lambda d: x_copy(d, lax.rem(x + d, NX)).wait_recv())
+    b1[...] = jnp.sum(bl1[...], axis=0) * (1.0 / 256.0)
+
+    def h_copy(slot, sender):
+        return remote(
+            b1, bl2.at[sender], h_ss.at[slot], h_rs.at[sender], f, seq_of(slot, zh)
+        )
+
+    repeat(1, 8, lambda d: h_copy(own_slot(d), me).start())
+    bl2[me] = b1[...]
+    repeat(1, 8, lambda d: h_copy(me, own_slot(d)).wait_recv())
+    for slot in range(8):
+        for head in range(GROUP):
+            brow[slot * GROUP + head] = bl2[slot, head : head + 1, :]
+        brow[QH + slot] = bl2[slot, 4:5, :]
+
     def z_copy(d, far, target):
-        there = lax.rem(zl + d, NZ)
-        return remote(
-            b0, bl1.at[target], z_ss.at[far * NZ + d], z_rs.at[target],
-            there * NX + x, seq_of(me, zh ^ far),
+        there = lax.rem(zl + d, NZ) * NX + x
+        return remote(
+            brow.at[pl.ds((there * WIDTH) // HD, 2)], bl3.at[target],
+            z_ss.at[far * NZ + d], z_rs.at[target], there, seq_of(me, zh ^ far),
         )
 
     def z_from(d, far):
         return z_copy(d, far, (zh ^ far) * NZ + lax.rem(zl + d, NZ))
 
+    repeat(0, NZ, lambda d: z_copy(d, 1, zi).start())
     repeat(1, NZ, lambda d: z_copy(d, 0, zi).start())
-    repeat(0, NZ, lambda d: z_copy(d, 1, zi).start())
+
+    def key_chunk(row):
+        rows = pl.ds(pl.multiple_of(row, TILE), TILE)
+        acc = jnp.zeros((TILE, HD), F32)
+        for head in range(GROUP):
+            span = slice(head * HALF, (head + 1) * HALF)
+            acc = acc + dot(ebuf[rows, span], qbuf[:, head * HD : (head + 1) * HD])
+        dkb[rows, :] = (acc * scaling).astype(BF16)
+
+    def key_other(i):
+        column = lax.rem(y + i, 4)
+        key_chunk(HALF + column * TILE)
+        dk_copy(column * 2, 1, me).start()
+        dk_copy(column * 2 + 1, 1, me).start()
+
+    repeat(0, 4, key_other)
 
     def dq_copy(slot, sender):
         return remote(
@@ -394,34 +426,8 @@
         own_sem.at[4],
     )
     own_dq.start()
-
-    bl1[zi] = b0[...]
-    repeat(1, NZ, lambda d: z_from(d, 0).wait_recv())
-    repeat(0, NZ, lambda d: z_from(d, 1).wait_recv())
-    b1[...] = jnp.sum(bl1[...], axis=0)
-
-    def x_copy(d, target):
-        return remote(
-            b1, bl2.at[target], x_ss.at[d], x_rs.at[target],
-            zl * NX + lax.rem(x + d, NX), s,
-        )
-
-    repeat(1, NX, lambda d: x_copy(d, x).start())
-    bl2[x] = b1[...]
-    repeat(1, NX, lambda d: x_copy(d, lax.rem(x + d, NX)).wait_recv())
-    b2[...] = jnp.sum(bl2[...], axis=0) * (1.0 / 256.0)
-
-    def h_copy(slot, sender):
-        return remote(
-            b2, bl3.at[sender], h_ss.at[slot], h_rs.at[sender], f, seq_of(slot, zh)
-        )
-
-    repeat(1, 8, lambda d: h_copy(own_slot(d), me).start())
-    bl3[me] = b2[...]
-    repeat(1, 8, lambda d: h_copy(me, own_slot(d)).wait_recv())
-    for slot in range(8):
-        bias_out[slot * 4 : slot * 4 + 4, :] = bl3[slot, 0:4, :]
-        bias_out[32 + slot : 33 + slot, :] = bl3[slot, 4:5, :]
+    repeat(0, 4, lambda i: key_chunk(i * TILE))
+    repeat(1, 8, lambda d: dk_copy(own_slot(d), 0, me).start())
 
     def finish(buf, landed, copy_of, out):
         landed[0, me] = buf[pl.ds(at128(me * TOK), TOK), :]
@@ -432,6 +438,12 @@
             out[:, slot * HD : (slot + 1) * HD] = total.astype(BF16)
 
     finish(dvb, dvl, dv_copy, dv_out)
+    bl3[zi] = brow[pl.ds((f * WIDTH) // HD, 2)]
+    repeat(1, NZ, lambda d: z_from(d, 0).wait_recv())
+    repeat(0, NZ, lambda d: z_from(d, 1).wait_recv())
+    total = jnp.sum(bl3[...], axis=0)
+    bias_out[0:1, :] = total[0]
+    bias_out[1:2, :] = total[1]
     finish(dkb, dkl, dk_copy, dk_out)
     own_dq.wait()
     repeat(1, 8, lambda d: dq_copy(me, own_slot(d)).wait_recv())
@@ -460,6 +472,20 @@
     repeat(1, NX, lambda d: x_copy(d, x).wait_send())
 
 
+def place(f_dq, f_dk, f_dv, f_bias, dq_out, dk_out, dv_out, bias_out):
+    dq_out[...] = f_dq[...]
+    dk_out[...] = f_dk[...]
+    dv_out[...] = f_dv[...]
+    first = lax.axis_index("fsdp") * WIDTH
+    pair = jnp.concatenate([f_bias[0:1, :], f_bias[1:2, :]], axis=1)
+    shift = lax.rem(first, HD)
+    piece = pair[:, 0:WIDTH]
+    for step in range(1, 4):
+        start = step * (HD // 4)
+        piece = jnp.where(shift == start, pair[:, start : start + WIDTH], piece)
+    bias_out[...] = piece
+
+
 def local(query, key, value, out_grad, pack_order, doc_ids):
     vmem = pl.BlockSpec(memory_space=pltpu.VMEM)
     hbm = pl.BlockSpec(memory_space=pl.ANY)
@@ -470,7 +496,7 @@
             jax.ShapeDtypeStruct((TOK, QH * HD), BF16),
             jax.ShapeDtypeStruct((TOK, KVH * HD), BF16),
             jax.ShapeDtypeStruct((TOK, KVH * HD), BF16),
-            jax.ShapeDtypeStruct((QH + KVH, HD), F32),
+            jax.ShapeDtypeStruct((2, HD), F32),
         ),
         in_specs=[hbm, hbm, hbm, hbm, vmem, vmem],
         out_specs=(hbm, vmem, vmem, vmem),
@@ -495,10 +521,10 @@
             pltpu.VMEM((2, 8, TOK, HD), BF16),
             pltpu.VMEM((8, 128), F32),
             pltpu.VMEM((8, 128), F32),
-            pltpu.VMEM((8, 128), F32),
-            pltpu.VMEM((2 * NZ, 8, 128), F32),
+            pltpu.VMEM((QH + KVH, 1, HD), F32),
             pltpu.VMEM((NX, 8, 128), F32),
             pltpu.VMEM((8, 8, 128), F32),
+            pltpu.VMEM((2 * NZ, 2, 1, HD), F32),
             dma((8,)), dma((8,)), dma((8,)), dma((8,)),
             dma((16,)), dma((16,)), dma((16,)), dma((16,)),
             dma((8,)), dma((8,)), dma((16,)), dma((16,)), dma((16,)), dma((16,)),
@@ -513,10 +539,19 @@
         ),
         name="attention_backward",
     )(query, key, value, out_grad, pack_order, doc_ids.reshape(1, FULL))
-    width = (QH + KVH) * HD // lax.axis_size("fsdp")
-    bias_grads = lax.dynamic_slice(
-        bias.reshape((QH + KVH) * HD), (lax.axis_index("fsdp") * width,), (width,)
-    )
+    query_grad, key_grad, value_grad, bias_grads = pl.pallas_call(
+        place,
+        out_shape=(
+            jax.ShapeDtypeStruct((TOK, QH * HD), BF16),
+            jax.ShapeDtypeStruct((TOK, KVH * HD), BF16),
+            jax.ShapeDtypeStruct((TOK, KVH * HD), BF16),
+            jax.ShapeDtypeStruct((1, WIDTH), F32),
+        ),
+        in_specs=[vmem] * 4,
+        out_specs=(vmem,) * 4,
+        name="place_gradients",
+    )(query_grad, key_grad, value_grad, bias)
+    bias_grads = bias_grads.reshape(WIDTH)
     return (query_grad, key_grad, value_grad, bias_grads)
 
 

time: 141 us -> 132 us (0.936)
  the two profiles are of different devices: /device:TPU:9 before, /device:TPU:33 now
where the time goes in v2:
time: 132 us
  Pallas kernels  131 us (99%)
    pallas_call x1, Pallas kernels, local(): pl.pallas_call(kernel, out_shape=(jax.ShapeDtypeStruct((TOK, QH * HD), BF...  129 us
    pallas_call x1, Pallas kernels, local(): pl.pallas_call(place, out_shape=(jax.ShapeDtypeStruct((TOK, QH * HD), BF1...  2.7 us

profile of v2, /device:TPU:33, one launch (start us, length us, event | category | flops | bytes accessed | tf_op | source)
XLA Modules:
  0.0 132.1 jit_solution(12091205241269898782)
XLA Ops:
  0.6 128.7 %attention_backward.1 = (bf16[128,4096]{1,0:T(8,128)(2,1)}, bf16[128,1024]{1,0:T(8,128)(2,1)}, bf16[128,1024]{1,0:T(8,128)(2,1)}, f32[2,128]{1,0:T(2,128)}) custom-call(bf16[128,4096]{1,0:T(8,128)(2,1)} %q_ref.1, bf16[128,1024]{1,0:T(8,128)(2,1)} %k_ref.1, bf16[128,1024]{1,0:T(8,128)(2,1)} %v_ref.1, bf16[128,4096]{1,0:T(8,128)(2,1)} %g_ref.1, ...), custom_call_target="tpu_custom_call" | custom-call | flops 12884901888 | bytes 8388608 | tf_op jit(solution)/shard_map/attention_backward/pallas_call | solution.py:493
  129.4 2.7 %place_gradients.1 = (bf16[128,4096]{1,0:T(8,128)(2,1)}, bf16[128,1024]{1,0:T(8,128)(2,1)}, bf16[128,1024]{1,0:T(8,128)(2,1)}, f32[1,160]{1,0:T(1,128)}) custom-call(bf16[128,4096]{1,0:T(8,128)(2,1)} %get-tuple-element.12.f_dq, bf16[128,1024]{1,0:T(8,128)(2,1)} %get-tuple-element.13.f_dk, bf16[128,1024]{1,0:T(8,128)(2,1)} %get-tuple-element.14.f_dv, ...), custom_call_target="tpu_custom_call" | custom-call | tf_op jit(solution)/shard_map/place_gradients/pallas_call | solution.py:542

commit v3 on v2

--- a/solution.py
+++ b/solution.py
@@ -431,11 +431,13 @@
 
     def finish(buf, landed, copy_of, out):
         landed[0, me] = buf[pl.ds(at128(me * TOK), TOK), :]
-        repeat(1, 8, lambda d: copy_of(me, 0, own_slot(d)).wait_recv())
-        repeat(0, 8, lambda d: copy_of(me, 1, other_slot(d)).wait_recv())
-        for slot in range(8):
+        for d in range(8):
+            slot = own_slot(d)
+            if d:
+                copy_of(me, 0, slot).wait_recv()
+            copy_of(me, 1, slot).wait_recv()
             total = landed[0, slot].astype(F32) + landed[1, slot].astype(F32)
-            out[:, slot * HD : (slot + 1) * HD] = total.astype(BF16)
+            out[:, pl.ds(at128(slot * HD), HD)] = total.astype(BF16)
 
     finish(dvb, dvl, dv_copy, dv_out)
     bl3[zi] = brow[pl.ds((f * WIDTH) // HD, 2)]
@@ -444,7 +446,6 @@
     total = jnp.sum(bl3[...], axis=0)
     bias_out[0:1, :] = total[0]
     bias_out[1:2, :] = total[1]
-    finish(dkb, dkl, dk_copy, dk_out)
     own_dq.wait()
     repeat(1, 8, lambda d: dq_copy(me, own_slot(d)).wait_recv())
 
@@ -470,6 +471,8 @@
     repeat(1, 8, near)
     repeat(0, 8, far)
     repeat(1, NX, lambda d: x_copy(d, x).wait_send())
+
+    finish(dkb, dkl, dk_copy, dk_out)
 
 
 def place(f_dq, f_dk, f_dv, f_bias, dq_out, dk_out, dv_out, bias_out):

time: 132 us -> 132 us (level)
  no operation moved by 1% of the time
where the time goes in v3:
time: 132 us
  Pallas kernels  131 us (99%)
    pallas_call x1, Pallas kernels, local(): pl.pallas_call(kernel, out_shape=(jax.ShapeDtypeStruct((TOK, QH * HD), BF...  128 us
    pallas_call x1, Pallas kernels, local(): pl.pallas_call(place, out_shape=(jax.ShapeDtypeStruct((TOK, QH * HD), BF1...  2.7 us

profile of v3, /device:TPU:33, one launch (start us, length us, event | category | flops | bytes accessed | tf_op | source)
XLA Modules:
  0.0 131.6 jit_solution(15104463593397555356)
XLA Ops:
  0.6 128.3 %attention_backward.1 = (bf16[128,4096]{1,0:T(8,128)(2,1)}, bf16[128,1024]{1,0:T(8,128)(2,1)}, bf16[128,1024]{1,0:T(8,128)(2,1)}, f32[2,128]{1,0:T(2,128)}) custom-call(bf16[128,4096]{1,0:T(8,128)(2,1)} %q_ref.1, bf16[128,1024]{1,0:T(8,128)(2,1)} %k_ref.1, bf16[128,1024]{1,0:T(8,128)(2,1)} %v_ref.1, bf16[128,4096]{1,0:T(8,128)(2,1)} %g_ref.1, ...), custom_call_target="tpu_custom_call" | custom-call | flops 12884901888 | bytes 8388608 | tf_op jit(solution)/shard_map/attention_backward/pallas_call | solution.py:496
  128.9 2.7 %place_gradients.1 = (bf16[128,4096]{1,0:T(8,128)(2,1)}, bf16[128,1024]{1,0:T(8,128)(2,1)}, bf16[128,1024]{1,0:T(8,128)(2,1)}, f32[1,160]{1,0:T(1,128)}) custom-call(bf16[128,4096]{1,0:T(8,128)(2,1)} %get-tuple-element.12.f_dq, bf16[128,1024]{1,0:T(8,128)(2,1)} %get-tuple-element.13.f_dk, bf16[128,1024]{1,0:T(8,128)(2,1)} %get-tuple-element.14.f_dv, ...), custom_call_target="tpu_custom_call" | custom-call | tf_op jit(solution)/shard_map/place_gradients/pallas_call | solution.py:545
